TPU v7x, 512 devices: a whole 4x4x16 slice. The times are simulated.
512 devices in a mesh: seq: 64 (over z_lo, x, core), batch: 8 (over z_hi, y).
Axes of the slice: x: 4, y: 4, z: 16 (z_hi: 2, z_lo: 8; z = z_hi * 8 + z_lo), core: 2. Of those that a mesh axis runs over, the one named last changes fastest.
Arguments:
- queries: bfloat16 [16, 4, 8192], P('batch'), may hold values from -45 to 45
- cache_levels: bfloat16 [16, 16384, 2048], P('batch', 'seq'), may hold values from -8 to 7, as said below
- scale_ids: int32 [16, 512], P('batch', 'seq'), may hold values from 0 to 15
- scale_table: float32 [16, 2048], P(None, 'batch'), may hold values from 0.05 to 0.5
- ctx_len: int32 [16, 64], P('batch', 'seq'), may hold values from 32 to 256, as said below
- span_rows: bfloat16 [16, 4096, 2048], P('batch', 'seq'), may hold values from -6 to 6
- span_len: int32 [16, 64], P('batch', 'seq'), may hold values from 16 to 64, as said below
- owners: int32 [16, 4096, 1], P('batch', 'seq'), may hold values from 0 to 63; in each aligned block of 64 rows (0 to 63, 64 to 127, ..., all dimensions but the last counted through in order) at most 2 rows name the same one
Outputs:
- attended: bfloat16 [16, 4, 8192], P('batch', None, 'seq')
- appended: bfloat16 [16, 8192, 2048], P('batch', 'seq')
Inputs may be any that keep to these rules, and one draw needn't show every extreme that they name: `cache_levels`: integer levels. `ctx_len`: some request has all 256 rows valid on some index of seq. `span_len`: some request has all 64 rows valid on some index of seq. `owners`: within the 64 block rows of one device of one request no owner is named more than 2 times.
All inputs are finite; a program needn't handle non-finite values.
Results may differ from a plain program's by a relative error of at most 0.012.
The roundings to bfloat16 on the way count: a program that leaves them out, or rounds other values in their place, can miss the bound.
Values may be sent and summed in bfloat16 or wider, within the bound.
A program may use at most 128 MiB of HBM per device.

v0:
```python
import jax
import jax.numpy as jnp
from jax import lax
from jax.sharding import PartitionSpec as P

HQ = 64
KVH = 8
HD = 128
G = 8
CAP = 2
GROUP = 32
NSCALE = 16


def combined_all(value, axis, join):
    pieces = jax.tree.map(lambda part: lax.all_gather(part, axis), value)
    head = jax.tree.map(lambda part: part[0], pieces)
    tail = jax.tree.map(lambda part: part[1:], pieces)
    running, _ = lax.scan(lambda running, piece: (join(running, piece), None), head, tail)
    return running


def hadamard(order):
    indices = jnp.arange(order, dtype=jnp.int32)
    common = jnp.bitwise_and(indices[:, None], indices[None, :])
    parity = jnp.zeros((order, order), jnp.int32)
    for bit_index in range(order.bit_length() - 1):
        parity = parity + jnp.bitwise_and(jnp.right_shift(common, bit_index), 1)
    signs = 1 - 2 * jnp.bitwise_and(parity, 1)
    return signs.astype(jnp.float32) / jnp.sqrt(jnp.float32(order))


def partial_softmax(grouped, all_rows, valid):
    request_count, row_count, row_width = all_rows.shape
    step_count = grouped.shape[1]
    key_rows = all_rows[:, :, : KVH * HD].reshape(request_count, row_count, KVH, HD)
    value_rows = all_rows[:, :, KVH * HD :].reshape(request_count, row_count, KVH, HD)
    scores = jnp.einsum("rskgd,rnkd->rskgn", grouped, key_rows, preferred_element_type=jnp.float32)
    scores = scores / jnp.sqrt(jnp.float32(HD))
    wide_mask = valid[:, None, None, None, :]
    masked = jnp.where(wide_mask, scores, jnp.float32(-1e30))
    row_max = jnp.max(masked, axis=-1)
    weights = jnp.where(wide_mask, jnp.exp(masked - row_max[..., None]), jnp.float32(0.0))
    weight_sum = jnp.sum(weights, axis=-1)
    accumulated = jnp.einsum(
        "rskgn,rnkd->rskgd",
        weights.astype(jnp.bfloat16),
        value_rows,
        preferred_element_type=jnp.float32,
    )
    return (
        row_max.reshape(request_count, step_count, HQ),
        weight_sum.reshape(request_count, step_count, HQ),
        accumulated.reshape(request_count, step_count, HQ, HD),
    )


def combine_partials(earlier, later):
    row_max = jnp.maximum(earlier[0], later[0])
    first_scale = jnp.exp(earlier[0] - row_max)
    second_scale = jnp.exp(later[0] - row_max)
    weight_sum = earlier[1] * first_scale + later[1] * second_scale
    accumulated = earlier[2] * first_scale[..., None] + later[2] * second_scale[..., None]
    return (row_max, weight_sum, accumulated)


def local(queries, cache_levels, scale_ids, scale_table, ctx_len, span_rows, span_len, owners):
    seq_count = lax.axis_size("seq")
    seq_rank = lax.axis_index("seq")
    request_count, slot_count, row_width = cache_levels.shape
    step_count = queries.shape[1]
    block_count = span_rows.shape[1]
    rotate = hadamard(HD)
    scale_full = lax.all_gather(scale_table, "batch", axis=1, tiled=True)
    query_f32 = queries.astype(jnp.float32).reshape(request_count, step_count, HQ, HD)
    query_rot = jnp.einsum(
        "rshd,de->rshe", query_f32, rotate, precision=lax.Precision.HIGHEST
    ).astype(jnp.bfloat16)
    grouped = query_rot.reshape(request_count, step_count, KVH, G, HD)
    choose = (scale_ids[..., None] == jnp.arange(NSCALE, dtype=jnp.int32)).astype(jnp.float32)
    scales = jnp.einsum("rbn,nc->rbc", choose, scale_full, precision=lax.Precision.HIGHEST)
    dequant = cache_levels.astype(jnp.float32).reshape(
        request_count, slot_count // GROUP, GROUP, row_width
    )
    dequant = (
        (dequant * scales[:, :, None, :])
        .reshape(request_count, slot_count, row_width)
        .astype(jnp.bfloat16)
    )
    cache_mask = jnp.arange(slot_count, dtype=jnp.int32)[None, :] < ctx_len
    row_mask = jnp.arange(block_count, dtype=jnp.int32)[None, :] < span_len
    kept_rows = jnp.where(row_mask[..., None], span_rows, jnp.zeros_like(span_rows))
    onehot = (owners[..., 0][..., None] == jnp.arange(seq_count, dtype=jnp.int32)).astype(jnp.int32)
    before = jnp.cumsum(onehot, axis=1) - onehot
    slot_rank = jnp.sum(before * onehot, axis=-1)
    slot_hot = (slot_rank[..., None] == jnp.arange(CAP, dtype=jnp.int32)).astype(jnp.int32)
    select = (onehot[..., :, None] * slot_hot[..., None, :]).astype(jnp.bfloat16)
    send_rows = jnp.einsum(
        "rjoc,rjw->rocw", select, kept_rows, preferred_element_type=jnp.float32
    ).astype(jnp.bfloat16)
    send_flags = jnp.einsum(
        "rjoc,rj->roc", select, row_mask.astype(jnp.bfloat16), preferred_element_type=jnp.float32
    ).astype(jnp.bfloat16)
    got_rows, got_flags = (
        lax.all_to_all(send_rows, "seq", split_axis=1, concat_axis=1, tiled=True),
        lax.all_to_all(send_flags, "seq", split_axis=1, concat_axis=1, tiled=True),
    )
    slot_flags = got_flags > 0
    appended = got_rows.reshape(request_count, seq_count * CAP, row_width)
    local_stats = partial_softmax(grouped, dequant, cache_mask)
    flags_flat = slot_flags.reshape(request_count, seq_count * CAP)
    extra_stats = partial_softmax(grouped, appended, flags_flat)
    joined = combine_partials(local_stats, extra_stats)
    local_heads = HQ // seq_count
    merged = combined_all(joined, "seq", combine_partials)
    weight_sum = lax.dynamic_slice_in_dim(merged[1], seq_rank * local_heads, local_heads, 2)
    accumulated = lax.dynamic_slice_in_dim(merged[2], seq_rank * local_heads, local_heads, 2)
    normed = accumulated / weight_sum[..., None]
    result = jnp.einsum("rshd,de->rshe", normed, rotate, precision=lax.Precision.HIGHEST)
    attended = result.reshape(request_count, step_count, local_heads * HD).astype(jnp.bfloat16)
    return (attended, appended)


def solution(mesh):
    return jax.shard_map(
        local,
        mesh=mesh,
        in_specs=(
            P("batch", None, None),
            P("batch", "seq", None),
            P("batch", "seq"),
            P(None, "batch"),
            P("batch", "seq"),
            P("batch", "seq", None),
            P("batch", "seq"),
            P("batch", "seq", None),
        ),
        out_specs=(P("batch", None, "seq"), P("batch", "seq", None)),
        check_vma=False,
    )
```

profile of v0, /device:TPU:1, one launch (start us, length us, event | category | flops | bytes accessed | tf_op | source)
XLA Modules:
  0.0 480.3 jit_solution(18390954105400856834)
XLA Ops:
  10.7 17.0 %all-to-all-start = ((bf16[2,64,2]{2,0,1:T(2,128)(2,1)}), bf16[2,64,2]{2,0,1:T(2,128)(2,1)S(1)}, u32[]{:S(2)}, u32[]{:S(2)}) async-start(bf16[2,64,2]{2,0,1:T(2,128)(2,1)} %bitcast.100), calls=%async_computation | async-start | bytes 65536 | tf_op jit(solution)/shard_map/all_to_all | solution.py:106
  27.8 1.5 convolution_convert_fusion
  29.3 2.1 copy.98
  31.4 8.7 %all-to-all-done = bf16[2,64,2]{2,0,1:T(2,128)(2,1)S(1)} async-done(((bf16[2,64,2]{2,0,1:T(2,128)(2,1)}), bf16[2,64,2]{2,0,1:T(2,128)(2,1)S(1)}, u32[]{:S(2)}, u32[]{:S(2)}) %all-to-all-start) | async-done | bytes 544 | tf_op jit(solution)/shard_map/all_to_all | solution.py:106
  40.1 4.7 all-to-all-start.1
  45.0 71.6 %all_gather.15 = f32[16,2048]{1,0:T(8,128)S(1)} all-gather(f32[16,256]{1,0:T(8,128)S(1)} %copy-done.3), channel_id=1, replica_groups=mesh['seq'=64,'batch'=8] {'batch'}, dimensions={1}, use_global_device_ids=true | all-gather | bytes 147456 | tf_op jit(solution)/shard_map/all_gather | solution.py:74
  116.9 2.1 fusion.3
  119.2 1.3 copy.91
  120.9 2.3 fusion.66
  123.9 1.5 convolution_bitcast_fusion.1
  128.2 1.9 fusion.65
  130.7 1.4 convolution_bitcast_fusion
  133.6 1.3 copy.114
  135.3 131.6 %all_gather.16 = f32[64,2,4,64]{3,2,1,0:T(4,128)S(1)} all-gather(f32[1,2,4,64]{3,2,1,0:T(4,128)S(1)} %bitcast.132), channel_id=1, replica_groups=mesh['seq'=64,'batch'=8] {'seq'}, dimensions={0}, use_global_device_ids=true | all-gather | bytes 133120 | tf_op jit(solution)/shard_map/all_gather | solution.py:16
  266.9 113.3 %all_gather.17 = f32[64,2,4,64]{3,2,1,0:T(4,128)S(1)} all-gather(f32[1,2,4,64]{3,2,1,0:T(4,128)S(1)} %bitcast.129), channel_id=1, replica_groups=mesh['seq'=64,'batch'=8] {'seq'}, dimensions={0}, use_global_device_ids=true | all-gather | bytes 133120 | tf_op jit(solution)/shard_map/all_gather | solution.py:16
  381.2 11.8 %slice.49 = f32[63,2,4,64,128]{4,3,2,1,0:T(8,128)} slice(f32[64,2,4,64,128]{4,3,2,1,0:T(8,128)} %all-gather.2.cloned.1.call-done), slice={[1:64], [0:2], [0:4], [0:64], [0:128]} | slice | bytes 33030144 | tf_op jit(solution)/shard_map/slice | solution.py:18
  393.1 79.3 %while.14 = (s32[]{:T(128)}, f32[2,4,64]{2,1,0:T(4,128)S(1)}, f32[2,4,64]{2,1,0:T(4,128)S(1)}, f32[2,4,64,128]{3,2,1,0:T(8,128)S(1)}, f32[63,2,4,64]{3,2,1,0:T(4...) while((s32[]{:T(128)}, f32[2,4,64]{2,1,0:T(4,128)S(1)}, ...), condition=%wide.region_7.8_spmd, body=%wide.region_6.7_spmd.sunk | while | flops 199682 | bytes 807013 | solution.py:19
  395.6 1.2 fusion.76
  396.8 1.2 fusion.76
  399.4 1.2 fusion.76
  400.6 1.2 fusion.76
  403.1 1.2 fusion.76
  405.7 1.2 fusion.76
  406.9 1.2 fusion.76
  409.4 1.2 fusion.76
  410.7 1.2 fusion.76
  413.2 1.2 fusion.76
  417.0 1.2 fusion.76
  419.5 1.2 fusion.76
  420.8 1.2 fusion.76
  423.3 1.2 fusion.76
  424.5 1.2 fusion.76
  427.1 1.2 fusion.76
  429.6 1.2 fusion.76
  430.8 1.2 fusion.76
  433.4 1.2 fusion.76
  434.6 1.2 fusion.76
  437.1 1.2 fusion.76
  440.9 1.2 fusion.76
  443.4 1.2 fusion.76
  444.7 1.2 fusion.76
  447.2 1.2 fusion.76
  448.5 1.2 fusion.76
  451.0 1.2 fusion.76
  453.5 1.2 fusion.76
  454.8 1.2 fusion.76
  457.3 1.2 fusion.76
  458.5 1.2 fusion.76
  (158 shorter events, 53.0 us)
Async XLA Ops:
  7.2 37.7 %copy-start.2 = (bf16[2,4,8192]{2,1,0:T(4,128)(2,1)S(1)}, bf16[2,4,8192]{2,1,0:T(4,128)(2,1)}, u32[]{:S(2)}) copy-start(bf16[2,4,8192]{2,1,0:T(4,128)(2,1)} %param.10) | copy-start | bytes 393220
  7.2 37.8 %copy-start.3 = (f32[16,256]{1,0:T(8,128)S(1)}, f32[16,256]{1,0:T(8,128)}, u32[]{:S(2)}) copy-start(f32[16,256]{1,0:T(8,128)} %param.13) | copy-start | bytes 49156
  7.2 109.4 %copy-start.4 = (s32[2,8]{1,0:T(2,128)S(1)}, s32[2,8]{1,0:T(2,128)}, u32[]{:S(2)}) copy-start(s32[2,8]{1,0:T(2,128)} %param.12) | copy-start | bytes 196
  10.7 29.3 %all-to-all-start = ((bf16[2,64,2]{2,0,1:T(2,128)(2,1)}), bf16[2,64,2]{2,0,1:T(2,128)(2,1)S(1)}, u32[]{:S(2)}, u32[]{:S(2)}) async-start(bf16[2,64,2]{2,0,1:T(2,128)(2,1)} %bitcast.100), calls=%async_computation | async-start | bytes 65536 | tf_op jit(solution)/shard_map/all_to_all | solution.py:106
  40.1 85.7 %all-to-all-start.1 = ((bf16[2,64,2,2048]{3,2,0,1:T(2,128)(2,1)}), bf16[2,64,2,2048]{3,2,0,1:T(2,128)(2,1)S(1)}, u32[]{:S(2)}, u32[]{:S(2)}) async-start(bf16[2,64,2,2048]{3,2,0,1:T(2,128)(2,1)} %copy.98), calls=%async_computation.1 | async-start | bytes 2097152 | tf_op jit(solution)/shard_map/all_to_all | solution.py:105
  44.8 335.5 %all-gather.2.cloned.1.call-start = ((), (), s32[]{:S(2)}) async-start(), calls=%async_computation.2 | async-start | bytes 17039360 | tf_op jit(solution)/shard_map/all_gather | solution.py:16
  119.0 1.9 copy-start.5
  120.8 3.0 copy-start.6
  126.9 6.2 %copy-start = (f32[2,4,8,8,256]{4,3,1,2,0:T(8,128)S(1)}, f32[2,4,8,8,256]{4,3,1,2,0:T(8,128)}, u32[]{:S(2)}) copy-start(f32[2,4,8,8,256]{4,3,1,2,0:T(8,128)} %get-tuple-element.83) | copy-start | bytes 1572868
  130.6 4.3 copy-start.1
Sparse Core Ops, SparseCore 0:
  133.1 163.5 all-gather.1
where the time goes:
time: 483 us; the launch traced here: 480 us
  blocking collectives  316 us (65%)
  other arithmetic  84.4 us (17%)
  local copies, waits for them, and re-layouts  23.2 us (5%)
  starting transfers between devices  21.8 us (5%)
  between operations  14.3 us (3%)
  matrix products  10.1 us (2%)
  waiting for transfers between devices  8.72 us (2%)
    all_gather x2, blocking collectives, combined_all(): pieces = jax.tree.map(lambda part: lax.all_gather(part, axis), value)  245 us
    add x64, other arithmetic, combine_partials(): earlier[2] * first_scale[..., None] + later[2] * second_scale[..., None]  77.3 us
    all_gather x1, blocking collectives, local(): scale_full = lax.all_gather(scale_table, 'batch', axis=1, tiled=True)  71.6 us
    all_to_all x1, starting transfers between devices, local(): lax.all_to_all(send_flags, 'seq', split_axis=1, concat_axis=1, tiled=True)  17 us
    slice x3, local copies, waits for them, and re-layouts, combined_all(): tail = jax.tree.map(lambda part: part[1:], pieces)  11.9 us
  transfers between devices with their start and end apart: 3, of which 1 were waited for; matrix products, arithmetic and copies ran while one was open for 3% of the time, Pallas kernels for 0%

commit v1 on v0

v1 whole, which is shorter than its diff:
```python
import functools

import jax
import jax.numpy as jnp
from jax import lax
from jax.experimental import pallas as pl
from jax.experimental.pallas import tpu as pltpu
from jax.sharding import PartitionSpec as P

HQ = 64
KVH = 8
HD = 128
G = 8
CAP = 2
GROUP = 32
NSCALE = 16
STEPS = 4
SLOT = 256
SPAN = 64
REQ = 2
WIDTH = 2 * KVH * HD
SEQ = 64
PLANE = 8
LAYERS = 8
BATCH_Y = 4
PIECE = WIDTH // 4
MESH = pl.DeviceIdType.MESH
F32 = jnp.float32
BF16 = jnp.bfloat16


def iota(shape, axis):
    return lax.broadcasted_iota(jnp.int32, shape, axis)


def hadamard_signs():
    common = jnp.bitwise_and(iota((HD, HD), 0), iota((HD, HD), 1))
    parity = jnp.zeros((HD, HD), jnp.int32)
    for bit in range(7):
        parity = parity + jnp.bitwise_and(jnp.right_shift(common, bit), 1)
    return (1 - 2 * jnp.bitwise_and(parity, 1)).astype(F32).astype(BF16)


def dot(a, b, contract=((1,), (0,))):
    return lax.dot_general(a, b, (contract, ((), ())), preferred_element_type=F32)


def exchange_kernel(
    q_ref, lev_hbm, ids_ref, tab_ref, ctx_ref, span_hbm, slen_ref, own_ref,
    land_hbm, part_hbm,
    lev, span, send, tbl, scales, qrot, mask, first_out, first_in, second_out,
    lev_sem, span_sem, own_sem, part_sem,
    a2a_send, a2a_recv, zh_send, zh_recv, y_send, y_recv,
    first_send, first_recv, second_send, second_recv,
):
    me = lax.axis_index("seq")
    layer, place = me // PLANE, lax.rem(me, PLANE)
    batch = lax.axis_index("batch")
    far, row = batch // BATCH_Y, lax.rem(batch, BATCH_Y)

    barrier = pltpu.get_barrier_semaphore()

    def greet(i, carry):
        pl.semaphore_signal(
            barrier, inc=1, device_id={"seq": lax.rem(me + i, SEQ)}, device_id_type=MESH
        )
        return carry

    lax.fori_loop(1, SEQ, greet, 0)
    partner = lax.rem(batch + BATCH_Y, 2 * BATCH_Y)
    pl.semaphore_signal(barrier, inc=1, device_id={"batch": partner}, device_id_type=MESH)
    sides = [far * BATCH_Y + lax.rem(row + i, BATCH_Y) for i in range(1, BATCH_Y)]
    for side in sides:
        pl.semaphore_signal(barrier, inc=1, device_id={"batch": side}, device_id_type=MESH)

    span_copy = pltpu.make_async_copy(span_hbm, span, span_sem)
    span_copy.start()
    lev_copy = pltpu.make_async_copy(lev_hbm, lev, lev_sem)
    lev_copy.start()

    owner_col = jnp.concatenate([own_ref[0], own_ref[1]], axis=0).astype(F32)
    above, along = iota((2 * SPAN, 2 * SPAN), 0), iota((2 * SPAN, 2 * SPAN), 1)
    owner_wide = jnp.broadcast_to(owner_col, (2 * SPAN, 2 * SPAN))
    owner_row = jnp.sum(jnp.where(above == along, owner_wide, 0.0), axis=0, keepdims=True)
    same = (owner_wide == owner_row) & (above < along) & (above // SPAN == along // SPAN)
    rank = jnp.sum(jnp.where(same, 1.0, 0.0), axis=0, keepdims=True)
    lane = iota((1, 2 * SPAN), 1)
    request = lane // SPAN
    kept = lax.rem(lane, SPAN) < jnp.where(request == 0, slen_ref[0, 0], slen_ref[1, 0])
    target = owner_row.astype(jnp.int32) * 16 + request * 8 + rank.astype(jnp.int32)
    target = jnp.concatenate(
        [jnp.where(kept, target + 2 * quarter, -1) for quarter in range(4)], axis=1
    )
    span_copy.wait()
    stacked = jnp.concatenate(
        [
            span[r, :, quarter * PIECE : (quarter + 1) * PIECE]
            for quarter in range(4)
            for r in range(REQ)
        ],
        axis=0,
    )
    for chunk in range(4):
        rows = iota((256, 512), 0) + chunk * 256
        pick = jnp.where(rows == target, 1.0, 0.0).astype(BF16)
        block = dot(pick, stacked).astype(BF16)
        send[chunk * 16 : (chunk + 1) * 16] = block.reshape(16, 16, PIECE)

    signs = hadamard_signs()
    root = jnp.float32(1.0) / jnp.sqrt(jnp.float32(HD))
    queries = jnp.concatenate([q_ref[0].astype(F32), q_ref[1].astype(F32)], axis=0)
    stacked_q = jnp.concatenate(
        [queries[:, h * HD : (h + 1) * HD] for h in range(HQ)], axis=0
    ).astype(BF16)
    qrot[...] = (dot(stacked_q, signs) * root).astype(BF16)

    keys = REQ * (SLOT + SPAN)
    wanted = lax.rem(iota((64, keys), 0) // STEPS, REQ)
    column = iota((64, keys), 1)
    in_slot = column < REQ * SLOT
    other = column - REQ * SLOT
    key_request = jnp.where(in_slot, column // SLOT, other // SPAN)
    position = jnp.where(in_slot, lax.rem(column, SLOT), lax.rem(other, SPAN))
    first = key_request == 0
    limit = jnp.where(
        in_slot,
        jnp.where(first, ctx_ref[0, 0], ctx_ref[1, 0]),
        jnp.where(first, slen_ref[0, 0], slen_ref[1, 0]),
    )
    mask[...] = jnp.where((wanted == key_request) & (position < limit), 1.0, 0.0)
    blocks = REQ * (SLOT // GROUP)
    group = jnp.zeros((blocks, 3 * NSCALE), jnp.int32)
    for r in range(REQ):
        for b in range(SLOT // GROUP):
            here = iota((blocks, 3 * NSCALE), 0) == r * (SLOT // GROUP) + b
            group = jnp.where(here, ids_ref[r, b], group)
    chosen = jnp.where(lax.rem(iota((blocks, 3 * NSCALE), 1), NSCALE) == group, 1.0, 0.0).astype(BF16)
    tbl[row, far] = tab_ref[...]

    pl.semaphore_wait(barrier, SEQ - 1 + BATCH_Y)

    far_copy = pltpu.make_async_remote_copy(
        src_ref=tbl.at[row, far], dst_ref=tbl.at[row, far], send_sem=zh_send, recv_sem=zh_recv,
        device_id={"batch": partner}, device_id_type=MESH,
    )
    far_copy.start()

    keep = pltpu.make_async_copy(send.at[me], land_hbm.at[me], own_sem)
    keep.start()

    def post(i, carry):
        step = i // PLANE
        to_layer = jnp.where(layer < LAYERS // 2, LAYERS - 1 - step, step)
        to = to_layer * PLANE + lax.rem(place + lax.rem(i, PLANE), PLANE)

        @pl.when(to != me)
        def _():
            pltpu.make_async_remote_copy(
                src_ref=send.at[to], dst_ref=land_hbm.at[me], send_sem=a2a_send, recv_sem=a2a_recv,
                device_id={"seq": to}, device_id_type=MESH,
            ).start()

        return carry

    lax.fori_loop(0, SEQ, post, 0)

    far_copy.wait()
    side_copies = [
        pltpu.make_async_remote_copy(
            src_ref=tbl.at[row], dst_ref=tbl.at[row], send_sem=y_send, recv_sem=y_recv,
            device_id={"batch": side}, device_id_type=MESH,
        )
        for side in sides
    ]
    for copy in side_copies:
        copy.start()
    lev_copy.wait()
    sides_all = pltpu.make_async_remote_copy(
        src_ref=tbl.at[pl.ds(0, BATCH_Y - 1)], dst_ref=tbl.at[pl.ds(0, BATCH_Y - 1)],
        send_sem=y_send, recv_sem=y_recv, device_id={"batch": partner}, device_id_type=MESH,
    )
    sides_all.wait_send()
    sides_all.wait_recv()

    for r in range(BATCH_Y):
        for f in range(2):
            piece = tbl[r, f]
            high = piece.astype(BF16)
            rest = piece - high.astype(F32)
            middle = rest.astype(BF16)
            low = (rest - middle.astype(F32)).astype(BF16)
            scales[r, f] = dot(chosen, jnp.concatenate([high, middle, low], axis=0))

    lane_stat = iota((64, HD), 1) < HD // 2

    def dequant(pair, half, base, part):
        pieces = []
        lanes = pl.ds(pl.multiple_of(base, HD), HD)
        for r in range(REQ):
            for b in range(SLOT // GROUP):
                at = r * (SLOT // GROUP) + b
                scale = scales[pair, part, at : at + 1, half * HD : (half + 1) * HD]
                level = lev[r, b * GROUP : (b + 1) * GROUP, lanes].astype(F32)
                pieces.append((level * scale).astype(BF16))
        for r in range(REQ):
            pieces.append(span[r, :, lanes])
        return jnp.concatenate(pieces, axis=0)

    def head_pair(pair, carry):
        for half in range(2):
            head = pair * 2 + half
            key_rows = dequant(pair, half, head * HD, 0)
            q = qrot[pl.ds(pl.multiple_of(head * 64, 64), 64), :]
            scores = dot(q, key_rows, ((1,), (1,))) * root
            scores = jnp.where(mask[...] > 0.0, scores, jnp.float32(-1e30))
            top = jnp.max(scores, axis=1, keepdims=True)
            weights = jnp.exp(scores - top)
            total = jnp.sum(weights, axis=1, keepdims=True)
            value_rows = dequant(pair, half, (KVH + head) * HD, 1)
            acc = dot(weights.astype(BF16), value_rows)
            stat = jnp.where(
                lane_stat, jnp.broadcast_to(top, (64, HD)), jnp.broadcast_to(total, (64, HD))
            )
            at = pl.ds(pl.multiple_of(head * 8, 8), 8)
            for g in range(G):
                first_out[g, 0, at, :] = acc[g * 8 : (g + 1) * 8]
                first_out[g, 1, at, :] = stat[g * 8 : (g + 1) * 8]
        return carry

    lax.fori_loop(0, KVH // 2, head_pair, 0)

    def first_post(i, carry):
        to = lax.rem(place + i, PLANE)
        pltpu.make_async_remote_copy(
            src_ref=first_out.at[to], dst_ref=first_in.at[place],
            send_sem=first_send, recv_sem=first_recv,
            device_id={"seq": layer * PLANE + to}, device_id_type=MESH,
        ).start()
        return carry

    lax.fori_loop(1, PLANE, first_post, 0)
    first_in[place] = first_out[place]
    first_all = pltpu.make_async_remote_copy(
        src_ref=first_out.at[pl.ds(0, PLANE - 1)], dst_ref=first_in.at[pl.ds(0, PLANE - 1)],
        send_sem=first_send, recv_sem=first_recv, device_id={"seq": me}, device_id_type=MESH,
    )
    first_all.wait_send()
    first_all.wait_recv()
    acc, stat = combine([(first_in[i, 0], first_in[i, 1]) for i in range(PLANE)])
    second_out[:, 0] = acc.reshape(LAYERS, 8, HD)
    second_out[:, 1] = stat.reshape(LAYERS, 8, HD)

    def second_post(i, carry):
        to = lax.rem(layer + i, LAYERS)
        pltpu.make_async_remote_copy(
            src_ref=second_out.at[to], dst_ref=part_hbm.at[layer],
            send_sem=second_send, recv_sem=second_recv,
            device_id={"seq": to * PLANE + place}, device_id_type=MESH,
        ).start()
        return carry

    lax.fori_loop(1, LAYERS, second_post, 0)
    own_part = pltpu.make_async_copy(second_out.at[layer], part_hbm.at[layer], part_sem)
    own_part.start()
    own_part.wait()
    second_all = pltpu.make_async_remote_copy(
        src_ref=second_out.at[pl.ds(0, LAYERS - 1)], dst_ref=part_hbm.at[pl.ds(0, LAYERS - 1)],
        send_sem=second_send, recv_sem=second_recv, device_id={"seq": me}, device_id_type=MESH,
    )
    second_all.wait_send()
    second_all.wait_recv()

    keep.wait()
    rows_all = pltpu.make_async_remote_copy(
        src_ref=send.at[pl.ds(0, SEQ - 1)], dst_ref=land_hbm.at[pl.ds(0, SEQ - 1)],
        send_sem=a2a_send, recv_sem=a2a_recv, device_id={"seq": me}, device_id_type=MESH,
    )
    rows_all.wait_send()
    rows_all.wait_recv()


def combine(parts):
    tops = [stat[:, 0:1] for _, stat in parts]
    top = functools.reduce(jnp.maximum, tops)
    acc = total = None
    for (values, stat), own_top in zip(parts, tops):
        factor = jnp.exp(own_top - top)
        scaled, weight = values * factor, stat[:, HD // 2 : HD // 2 + 1] * factor
        acc = scaled if acc is None else acc + scaled
        total = weight if total is None else total + weight
    shape = acc.shape
    left = iota(shape, 1) < HD // 2
    return acc, jnp.where(left, jnp.broadcast_to(top, shape), jnp.broadcast_to(total, shape))


def finish_kernel(land_hbm, part_ref, att_ref, app_hbm, land, app, in_sems, out_sems):
    chunks = SEQ // 8
    for c in range(chunks):
        pltpu.make_async_copy(
            land_hbm.at[pl.ds(c * 8, 8)], land.at[pl.ds(c * 8, 8)], in_sems.at[c]
        ).start()
    to = iota((128, 128), 0)
    request, quarter = to // 64, lax.rem(to // 16, 4)
    source, rank = lax.rem(to // 2, 8), lax.rem(to, 2)
    wanted = source * 16 + request * 8 + quarter * 2 + rank
    move = jnp.where(iota((128, 128), 1) == wanted, 1.0, 0.0).astype(BF16)

    acc, stat = combine([(part_ref[i, 0], part_ref[i, 1]) for i in range(LAYERS)])
    normed = acc / stat[:, HD // 2 : HD // 2 + 1]
    signs = hadamard_signs()
    high = normed.astype(BF16)
    rest = normed - high.astype(F32)
    middle = rest.astype(BF16)
    low = (rest - middle.astype(F32)).astype(BF16)
    root = jnp.float32(1.0) / jnp.sqrt(jnp.float32(HD))
    turned = (dot(low, signs) + dot(middle, signs) + dot(high, signs)) * root
    att_ref[0] = turned[0:STEPS].astype(BF16)
    att_ref[1] = turned[STEPS : 2 * STEPS].astype(BF16)

    def out_copy(c):
        rows = pl.ds(c * 16, 16)
        return pltpu.make_async_copy(app.at[:, rows, :], app_hbm.at[:, rows, :], out_sems.at[c])

    for c in range(chunks):
        pltpu.make_async_copy(
            land_hbm.at[pl.ds(c * 8, 8)], land.at[pl.ds(c * 8, 8)], in_sems.at[c]
        ).wait()
        block = land[c * 8 : (c + 1) * 8].reshape(128, PIECE)
        moved = dot(move, block).astype(BF16)
        for r in range(REQ):
            for q in range(4):
                start = r * 64 + q * 16
                app[r, c * 16 : (c + 1) * 16, q * PIECE : (q + 1) * PIECE] = moved[start : start + 16]
        out_copy(c).start()
    for c in range(chunks):
        out_copy(c).wait()


def local(queries, cache_levels, scale_ids, scale_table, ctx_len, span_rows, span_len, owners):
    vmem, smem = pl.BlockSpec(memory_space=pltpu.VMEM), pl.BlockSpec(memory_space=pltpu.SMEM)
    anywhere = pl.BlockSpec(memory_space=pl.ANY)
    dma = pltpu.SemaphoreType.DMA
    landed, parts = pl.pallas_call(
        exchange_kernel,
        out_shape=(
            jax.ShapeDtypeStruct((SEQ, 16, PIECE), BF16),
            jax.ShapeDtypeStruct((LAYERS, 2, 8, HD), F32),
        ),
        in_specs=[vmem, anywhere, smem, vmem, smem, anywhere, smem, vmem],
        out_specs=(anywhere, anywhere),
        scratch_shapes=[
            pltpu.VMEM((REQ, SLOT, WIDTH), BF16),
            pltpu.VMEM((REQ, SPAN, WIDTH), BF16),
            pltpu.VMEM((SEQ, 16, PIECE), BF16),
            pltpu.VMEM((BATCH_Y, 2, NSCALE, 256), F32),
            pltpu.VMEM((BATCH_Y, 2, REQ * (SLOT // GROUP), 256), F32),
            pltpu.VMEM((HQ * 8, HD), BF16),
            pltpu.VMEM((64, REQ * (SLOT + SPAN)), F32),
            pltpu.VMEM((PLANE, 2, 64, HD), F32),
            pltpu.VMEM((PLANE, 2, 64, HD), F32),
            pltpu.VMEM((LAYERS, 2, 8, HD), F32),
        ]
        + [dma] * 14,
        compiler_params=pltpu.CompilerParams(
            collective_id=0, has_side_effects=True, vmem_limit_bytes=40 * 2**20
        ),
        cost_estimate=pl.CostEstimate(
            flops=2 * 10**9, bytes_accessed=5 * 2**20, transcendentals=400000
        ),
        name="exchange",
    )(queries, cache_levels, scale_ids, scale_table, ctx_len, span_rows, span_len, owners)
    return pl.pallas_call(
        finish_kernel,
        out_shape=(
            jax.ShapeDtypeStruct((REQ, STEPS, HD), BF16),
            jax.ShapeDtypeStruct((REQ, SEQ * CAP, WIDTH), BF16),
        ),
        in_specs=[anywhere, vmem],
        out_specs=(vmem, anywhere),
        scratch_shapes=[
            pltpu.VMEM((SEQ, 16, PIECE), BF16),
            pltpu.VMEM((REQ, SEQ * CAP, WIDTH), BF16),
            dma((8,)),
            dma((8,)),
        ],
        compiler_params=pltpu.CompilerParams(vmem_limit_bytes=40 * 2**20),
        name="finish",
    )(landed, parts)


def solution(mesh):
    return jax.shard_map(
        local,
        mesh=mesh,
        in_specs=(
            P("batch", None, None),
            P("batch", "seq", None),
            P("batch", "seq"),
            P(None, "batch"),
            P("batch", "seq"),
            P("batch", "seq", None),
            P("batch", "seq"),
            P("batch", "seq", None),
        ),
        out_specs=(P("batch", None, "seq"), P("batch", "seq", None)),
        check_vma=False,
    )
```

time: 483 us -> 80.8 us (0.17)
  blocking collectives: 316 us -> 0 us
  other arithmetic: 84.4 us -> 0 us
  Pallas kernels: 0 us -> 72.6 us
  starting transfers between devices: 21.8 us -> 0 us
  local copies, waits for them, and re-layouts: 23.2 us -> 7.18 us
  between operations: 14.3 us -> 0.66 us
  matrix products: 10.1 us -> 0 us
  waiting for transfers between devices: 8.72 us -> 0 us
    all_gather x3 -> x0, blocking collectives: 316 us -> none  [the longest x2 245 us: combined_all(): pieces = jax.tree.map(lambda part: lax.all_gather(part, axis), value)]
    add x128 -> x0, other arithmetic: 79 us -> none  [the longest x64 77.3 us: combine_partials(): earlier[2] * first_scale[..., None] + later[2] * second_scale[..., None]]
    pallas_call x0 -> x2, Pallas kernels: none -> 72.6 us  [the longest x1 68 us: local(): pl.pallas_call(exchange_kernel, out_shape=(jax.ShapeDtypeStruct((SEQ, 16,...]
    all_to_all x2 -> x0, starting transfers between devices: 21.8 us -> none  [the longest x1 17 us: local(): lax.all_to_all(send_flags, 'seq', split_axis=1, concat_axis=1, tiled=True)]
    slice x9 -> x0, local copies, waits for them, and re-layouts: 15.7 us -> none  [the longest x3 11.9 us: combined_all(): tail = jax.tree.map(lambda part: part[1:], pieces)]
    dot_general x9 -> x0, matrix products: 10.1 us -> none  [the longest x2 4.16 us: partial_softmax(): jnp.einsum('rskgd,rnkd->rskgn', grouped, key_rows, preferred_element_type...]
    all_to_all x2 -> x0, waiting for transfers between devices: 8.69 us -> none  [the longest x1 8.68 us: local(): lax.all_to_all(send_flags, 'seq', split_axis=1, concat_axis=1, tiled=True)]
    unnamed x15 -> x13, local copies, waits for them, and re-layouts: 1.37 us -> 7.18 us
  transfers between devices with their start and end apart: 3 -> 0, of which waited for: 1 -> 0; matrix products, arithmetic and copies ran while one was open for 3% -> 0% of each run, Pallas kernels for 0% -> 0%
where the time goes in v1:
time: 80.8 us; the launch traced here: 80.4 us
  Pallas kernels  72.6 us (90%)
  local copies, waits for them, and re-layouts  7.18 us (9%)
    pallas_call x1, Pallas kernels, local(): pl.pallas_call(exchange_kernel, out_shape=(jax.ShapeDtypeStruct((SEQ, 16,...  68 us
    unnamed x13, local copies, waits for them, and re-layouts  7.18 us
    pallas_call x1, Pallas kernels, local(): pl.pallas_call(finish_kernel, out_shape=(jax.ShapeDtypeStruct((REQ, STEPS...  4.55 us

profile of v1, /device:TPU:1, one launch (start us, length us, event | category | flops | bytes accessed | tf_op | source)
XLA Modules:
  0.0 80.4 jit_solution(8104865112182733707)
XLA Ops:
  0.6 0.7 copy.10.ctx_ref
  1.4 0.7 copy.11.slen_ref
  2.1 0.8 copy.12.own_ref
  2.9 0.0 copy-start
  2.9 1.6 %copy-done = bf16[2,256,2048]{2,1,0:T(8,128)(2,1)S(1)} copy-done((bf16[2,256,2048]{2,1,0:T(8,128)(2,1)S(1)}, bf16[2,256,2048]{2,1,0:T(8,128)(2,1)}, u32[]{:S(2)}) %copy-start) | copy-done | bytes 2097176
  4.5 0.0 copy-start.1
  4.5 1.0 %copy-done.1 = bf16[2,64,2048]{2,1,0:T(8,128)(2,1)S(1)} copy-done((bf16[2,64,2048]{2,1,0:T(8,128)(2,1)S(1)}, bf16[2,64,2048]{2,1,0:T(8,128)(2,1)}, u32[]{:S(2)}) %copy-start.1) | copy-done | bytes 524312
  5.5 0.0 copy-start.2
  5.5 0.9 %copy-done.2 = bf16[2,4,8192]{2,1,0:T(4,128)(2,1)S(1)} copy-done((bf16[2,4,8192]{2,1,0:T(4,128)(2,1)S(1)}, bf16[2,4,8192]{2,1,0:T(4,128)(2,1)}, u32[]{:S(2)}) %copy-start.2) | copy-done | bytes 131096
  6.4 0.0 copy-start.3
  6.4 0.7 copy-done.3
  7.2 0.0 copy-start.4
  7.2 0.7 copy-done.4
  7.8 68.0 %exchange.1 = (bf16[64,16,512]{2,1,0:T(8,128)(2,1)S(1)}, f32[8,2,8,128]{3,2,1,0:T(8,128)S(1)}) custom-call(bf16[2,4,8192]{2,1,0:T(4,128)(2,1)S(1)} %copy-done.2, bf16[2,256,2048]{2,1,0:T(8,128)(2,1)S(1)} %copy-done, s32[2,8]{1,0:T(2,128)S(1)} %copy-done.4, f32[16,256]{1,0:T(8,128)S(1)} %copy-done.3, s32[2,1]{1,0:T(2,128)S(1)} %copy.10.ctx_ref, ...), custom_call_target="tpu_custom_call" | custom-call | flops 2000000000 | bytes 5242880 | tf_op jit(solution)/shard_map/exchange/pallas_call | solution.py:343
  75.9 4.6 %finish.1 = (bf16[2,4,128]{2,1,0:T(4,128)(2,1)}, bf16[2,128,2048]{2,1,0:T(8,128)(2,1)}) custom-call(bf16[64,16,512]{2,1,0:T(8,128)(2,1)S(1)} %get-tuple-element.4.land_hbm, f32[8,2,8,128]{3,2,1,0:T(8,128)S(1)} %get-tuple-element.5.part_ref), custom_call_target="tpu_custom_call" | custom-call | tf_op jit(solution)/shard_map/finish/pallas_call | solution.py:372
Async XLA Ops:
  2.9 1.6 %copy-start = (bf16[2,256,2048]{2,1,0:T(8,128)(2,1)S(1)}, bf16[2,256,2048]{2,1,0:T(8,128)(2,1)}, u32[]{:S(2)}) copy-start(bf16[2,256,2048]{2,1,0:T(8,128)(2,1)} %lev_hbm.1) | copy-start | bytes 6291460
  4.5 1.0 %copy-start.1 = (bf16[2,64,2048]{2,1,0:T(8,128)(2,1)S(1)}, bf16[2,64,2048]{2,1,0:T(8,128)(2,1)}, u32[]{:S(2)}) copy-start(bf16[2,64,2048]{2,1,0:T(8,128)(2,1)} %span_hbm.1) | copy-start | bytes 1572868
  5.5 0.9 %copy-start.2 = (bf16[2,4,8192]{2,1,0:T(4,128)(2,1)S(1)}, bf16[2,4,8192]{2,1,0:T(4,128)(2,1)}, u32[]{:S(2)}) copy-start(bf16[2,4,8192]{2,1,0:T(4,128)(2,1)} %q_ref.1) | copy-start | bytes 393220
  6.4 0.7 copy-start.3
  7.2 0.7 copy-start.4

commit v2 on v1

v2 whole, which is shorter than its diff:
```python
import functools

import jax
import jax.numpy as jnp
from jax import lax
from jax.experimental import pallas as pl
from jax.experimental.pallas import tpu as pltpu
from jax.sharding import PartitionSpec as P

HQ = 64
KVH = 8
HD = 128
G = 8
CAP = 2
GROUP = 32
NSCALE = 16
STEPS = 4
SLOT = 256
SPAN = 64
REQ = 2
WIDTH = 2 * KVH * HD
SEQ = 64
PLANE = 8
LAYERS = 8
BATCH_Y = 4
PIECE = WIDTH // 4
VMEM = 60 * 2**20
MESH = pl.DeviceIdType.MESH
F32 = jnp.float32
BF16 = jnp.bfloat16


def iota(shape, axis):
    return lax.broadcasted_iota(jnp.int32, shape, axis)


def hadamard_signs():
    common = jnp.bitwise_and(iota((HD, HD), 0), iota((HD, HD), 1))
    parity = jnp.zeros((HD, HD), jnp.int32)
    for bit in range(7):
        parity = parity + jnp.bitwise_and(jnp.right_shift(common, bit), 1)
    return (1 - 2 * jnp.bitwise_and(parity, 1)).astype(F32).astype(BF16)


def dot(a, b, contract=((1,), (0,))):
    return lax.dot_general(a, b, (contract, ((), ())), preferred_element_type=F32)


def as_column(row, hot):
    return jnp.sum(jnp.where(hot, jnp.broadcast_to(row, hot.shape), 0.0), axis=1, keepdims=True)


def join(stats):
    tops = jnp.concatenate([stat[0:1] for stat in stats], axis=0)
    totals = jnp.concatenate([stat[1:2] for stat in stats], axis=0)
    top = jnp.max(tops, axis=0, keepdims=True)
    factors = jnp.exp(tops - top)
    return factors, top, jnp.sum(totals * factors, axis=0, keepdims=True)


def exchange_kernel(
    q_hbm, lev_hbm, ids_ref, tab_hbm, ctx_ref, span_hbm, slen_ref, own_ref,
    land_hbm, att_ref,
    q_ref, lev, span, send, tbl, scales, qrot, mask,
    first_out, first_in, first_stat, first_got, second_out, second_in, second_stat, second_got,
    q_sem, tab_sem, lev_sem, span_sem, own_sem,
    a2a_send, a2a_recv, far_send, far_recv, near_send, near_recv, side_send, side_recv,
    first_send, first_recv, first_stat_send, first_stat_recv,
    second_send, second_recv, second_stat_send, second_stat_recv,
    ready,
):
    me = lax.axis_index("seq")
    layer, place = me // PLANE, lax.rem(me, PLANE)
    batch = lax.axis_index("batch")
    far, row = batch // BATCH_Y, lax.rem(batch, BATCH_Y)
    partner = lax.rem(batch + BATCH_Y, 2 * BATCH_Y)
    sides = [far * BATCH_Y + lax.rem(row + i, BATCH_Y) for i in range(1, BATCH_Y)]
    lower = layer < LAYERS // 2

    def loop(start, stop, body):
        def step(i, carry):
            body(i)
            return carry

        lax.fori_loop(start, stop, step, 0)

    barrier = pltpu.get_barrier_semaphore()

    def greet(to):
        pl.semaphore_signal(barrier, inc=1, device_id=to, device_id_type=MESH)

    loop(1, PLANE, lambda i: greet({"seq": layer * PLANE + lax.rem(place + i, PLANE)}))
    for side in sides:
        greet({"batch": side})
    pl.when(far == 0)(lambda: greet({"batch": partner}))
    loop((layer + 1) * PLANE, SEQ, lambda i: greet({"seq": i}))

    span_copy = pltpu.make_async_copy(span_hbm, span, span_sem)
    span_copy.start()
    tab_copy = pltpu.make_async_copy(tab_hbm, tbl.at[far, row], tab_sem)
    tab_copy.start()
    q_copy = pltpu.make_async_copy(q_hbm, q_ref, q_sem)
    q_copy.start()
    lev_copy = pltpu.make_async_copy(lev_hbm, lev, lev_sem)
    lev_copy.start()

    owner_row = jnp.concatenate([own_ref[0], own_ref[1]], axis=1).astype(F32)
    above, along = iota((2 * SPAN, 2 * SPAN), 0), iota((2 * SPAN, 2 * SPAN), 1)
    owner_wide = jnp.broadcast_to(owner_row, (2 * SPAN, 2 * SPAN))
    owner_col = jnp.sum(jnp.where(above == along, owner_wide, 0.0), axis=1, keepdims=True)
    same = (owner_wide == owner_col) & (above < along) & (above // SPAN == along // SPAN)
    rank = jnp.sum(jnp.where(same, 1.0, 0.0), axis=0, keepdims=True)
    lane = iota((1, 2 * SPAN), 1)
    request = lane // SPAN
    kept = lax.rem(lane, SPAN) < jnp.where(request == 0, slen_ref[0, 0], slen_ref[0, 1])
    target = owner_row.astype(jnp.int32) * 16 + request * 8 + rank.astype(jnp.int32)
    target = jnp.concatenate(
        [jnp.where(kept, target + 2 * quarter, -1) for quarter in range(4)], axis=1
    )
    span_copy.wait()
    stacked = jnp.concatenate(
        [
            span[r, :, quarter * PIECE : (quarter + 1) * PIECE]
            for quarter in range(4)
            for r in range(REQ)
        ],
        axis=0,
    )
    for to_layer in range(LAYERS):
        rows = iota((16 * PLANE, REQ * SPAN * 4), 0) + to_layer * (16 * PLANE)
        pick = jnp.where(rows == target, 1.0, 0.0).astype(BF16)
        block = dot(pick, stacked).astype(BF16)
        send[pl.ds(to_layer * PLANE, PLANE)] = block.reshape(PLANE, 16, PIECE)

    pl.semaphore_wait(barrier, PLANE - 1 + BATCH_Y - 1 + far + layer * PLANE)

    loop(
        0,
        layer,
        lambda i: pl.semaphore_signal(
            ready.at[layer], inc=1, device_id={"seq": i * PLANE + place}, device_id_type=MESH
        ),
    )

    tab_copy.wait()
    far_copy = pltpu.make_async_remote_copy(
        src_ref=tbl.at[far, row], dst_ref=tbl.at[far, row], send_sem=far_send, recv_sem=far_recv,
        device_id={"batch": partner}, device_id_type=MESH,
    )
    pl.when(far == 1)(far_copy.start)

    def to_sides(half, send_sem, recv_sem):
        for side in sides:
            pltpu.make_async_remote_copy(
                src_ref=tbl.at[half, row], dst_ref=tbl.at[half, row],
                send_sem=send_sem, recv_sem=recv_sem,
                device_id={"batch": side}, device_id_type=MESH,
            ).start()

    def from_sides(send_sem, recv_sem):
        some = tbl.at[0, pl.ds(0, BATCH_Y - 1)]
        every = pltpu.make_async_remote_copy(
            src_ref=some, dst_ref=some, send_sem=send_sem, recv_sem=recv_sem,
            device_id={"batch": partner}, device_id_type=MESH,
        )
        every.wait_send()
        every.wait_recv()

    to_sides(far, near_send, near_recv)

    def await_layer(to_layer):
        pl.when(to_layer > layer)(lambda: pl.semaphore_wait(ready.at[to_layer], 1))

    def send_rows(to_layer, start=0):
        def one(i):
            to = to_layer * PLANE + lax.rem(place + i, PLANE)
            pltpu.make_async_remote_copy(
                src_ref=send.at[to], dst_ref=land_hbm.at[me], send_sem=a2a_send, recv_sem=a2a_recv,
                device_id={"seq": to}, device_id_type=MESH,
            ).start()

        loop(start, PLANE, one)

    def post(to_layer):
        await_layer(to_layer)
        send_rows(to_layer)

    half = LAYERS // 2
    base = layer // half * half
    across = [jnp.where(lower, half + i, half - 1 - i) for i in (0, 3, 1, 2)]
    beside = [base + lax.rem(layer + i, half) for i in range(1, half)]

    rest = [across[2], beside[0], beside[1], across[3], beside[2]]
    post(across[0])
    post(across[1])
    send_rows(layer, 1)
    keep = pltpu.make_async_copy(send.at[me], land_hbm.at[me], own_sem)
    keep.start()

    @pl.when(far == 1)
    def _():
        for to_layer in rest[: 5]:
            post(to_layer)

    signs = hadamard_signs()
    root = jnp.float32(1.0) / jnp.sqrt(jnp.float32(HD))
    q_copy.wait()
    queries = jnp.concatenate([q_ref[0].astype(F32), q_ref[1].astype(F32)], axis=0)
    stacked_q = jnp.concatenate(
        [queries[:, h * HD : (h + 1) * HD] for h in range(HQ)], axis=0
    ).astype(BF16)
    qrot[...] = (dot(stacked_q, signs) * root).astype(BF16)

    keys = REQ * (SLOT + SPAN)
    wanted = lax.rem(iota((64, keys), 0) // STEPS, REQ)
    column = iota((64, keys), 1)
    in_slot = column < REQ * SLOT
    other = column - REQ * SLOT
    key_request = jnp.where(in_slot, column // SLOT, other // SPAN)
    position = jnp.where(in_slot, lax.rem(column, SLOT), lax.rem(other, SPAN))
    first = key_request == 0
    limit = jnp.where(
        in_slot,
        jnp.where(first, ctx_ref[0, 0], ctx_ref[0, 1]),
        jnp.where(first, slen_ref[0, 0], slen_ref[0, 1]),
    )
    mask[...] = jnp.where((wanted == key_request) & (position < limit), 1.0, 0.0)
    blocks = REQ * (SLOT // GROUP)
    group = jnp.zeros((blocks, 3 * NSCALE), jnp.int32)
    for r in range(REQ):
        for b in range(SLOT // GROUP):
            here = iota((blocks, 3 * NSCALE), 0) == r * (SLOT // GROUP) + b
            group = jnp.where(here, ids_ref[r, b], group)
    chosen = jnp.where(lax.rem(iota((blocks, 3 * NSCALE), 1), NSCALE) == group, 1.0, 0.0).astype(BF16)

    far_copy.wait_recv()

    @pl.when(far == 0)
    def _():
        far_copy.start()
        for to_layer in rest[: 3]:
            post(to_layer)

    to_sides(1 - far, side_send, side_recv)
    from_sides(near_send, near_recv)
    from_sides(side_send, side_recv)

    for f in range(2):
        for r in range(BATCH_Y):
            piece = tbl[f, r]
            high = piece.astype(BF16)
            remain = piece - high.astype(F32)
            middle = remain.astype(BF16)
            low = (remain - middle.astype(F32)).astype(BF16)
            scales[f, r] = dot(chosen, jnp.concatenate([high, middle, low], axis=0))
    lev_copy.wait()

    lane = iota((64, HD), 1)
    sub = lax.rem(iota((64, HD), 0), 8)

    def dequant(pair, half, base, part):
        pieces = []
        lanes = pl.ds(pl.multiple_of(base, HD), HD)
        for r in range(REQ):
            for b in range(SLOT // GROUP):
                at = r * (SLOT // GROUP) + b
                scale = scales[part, pair, at : at + 1, half * HD : (half + 1) * HD]
                level = lev[r, b * GROUP : (b + 1) * GROUP, lanes].astype(F32)
                pieces.append((level * scale).astype(BF16))
        for r in range(REQ):
            pieces.append(span[r, :, lanes])
        return jnp.concatenate(pieces, axis=0)

    def head_pair(pair, carry):
        tops, totals = carry
        for half in range(2):
            head = pair * 2 + half
            key_rows = dequant(pair, half, head * HD, 0)
            q = qrot[pl.ds(pl.multiple_of(head * 64, 64), 64), :]
            scores = dot(q, key_rows, ((1,), (1,))) * root
            scores = jnp.where(mask[...] > 0.0, scores, jnp.float32(-1e30))
            top = jnp.max(scores, axis=1, keepdims=True)
            weights = jnp.exp(scores - top)
            total = jnp.sum(weights, axis=1, keepdims=True)
            value_rows = dequant(pair, half, (KVH + head) * HD, 1)
            acc = dot(weights.astype(BF16), value_rows)
            hot = lane == head * 8 + sub
            tops = tops + jnp.sum(jnp.where(hot, top, 0.0).reshape(G, 8, HD), axis=1)
            totals = totals + jnp.sum(jnp.where(hot, total, 0.0).reshape(G, 8, HD), axis=1)
            at = pl.ds(pl.multiple_of(head * 8, 8), 8)
            for g in range(G):
                first_out[g, at, :] = acc[g * 8 : (g + 1) * 8]
        return tops, totals

    zeros = jnp.zeros((G, HD), F32)
    tops, totals = lax.fori_loop(0, KVH // 2, head_pair, (zeros, zeros))
    for g in range(G):
        first_stat[g, 0:1] = tops[g : g + 1]
        first_stat[g, 1:2] = totals[g : g + 1]

    def first_post(i):
        to = lax.rem(place + i, PLANE)
        for out, into, send_sem, recv_sem in (
            (first_out, first_in, first_send, first_recv),
            (first_stat, first_got, first_stat_send, first_stat_recv),
        ):
            pltpu.make_async_remote_copy(
                src_ref=out.at[to], dst_ref=into.at[place], send_sem=send_sem, recv_sem=recv_sem,
                device_id={"seq": layer * PLANE + to}, device_id_type=MESH,
            ).start()

    def wait_all(out, into, count, send_sem, recv_sem):
        every = pltpu.make_async_remote_copy(
            src_ref=out.at[pl.ds(0, count)], dst_ref=into.at[pl.ds(0, count)],
            send_sem=send_sem, recv_sem=recv_sem, device_id={"seq": me}, device_id_type=MESH,
        )
        every.wait_send()
        every.wait_recv()

    loop(1, PLANE, first_post)
    first_in[place] = first_out[place]
    first_got[place] = first_stat[place]
    wait_all(first_out, first_in, PLANE - 1, first_send, first_recv)
    wait_all(first_stat, first_got, PLANE - 1, first_stat_send, first_stat_recv)
    factors, top, total = join([first_got[i] for i in range(PLANE)])
    hot = lane == iota((64, HD), 0)
    acc = None
    for i in range(PLANE):
        term = first_in[i] * as_column(factors[i : i + 1], hot)
        acc = term if acc is None else acc + term
    second_out[...] = acc.reshape(LAYERS, 8, HD)
    second_stat[0, 0:1] = top
    second_stat[0, 1:2] = total

    def second_post(i):
        to = lax.rem(layer + i, LAYERS)
        for out, into, send_sem, recv_sem in (
            (second_out.at[to], second_in, second_send, second_recv),
            (second_stat.at[0], second_got, second_stat_send, second_stat_recv),
        ):
            pltpu.make_async_remote_copy(
                src_ref=out, dst_ref=into.at[layer], send_sem=send_sem, recv_sem=recv_sem,
                device_id={"seq": to * PLANE + place}, device_id_type=MESH,
            ).start()

    @pl.when(far == 0)
    def _():
        for to_layer in rest[3 :]:
            await_layer(to_layer)

    loop(1, LAYERS, second_post)

    @pl.when(far == 0)
    def _():
        for to_layer in rest[3 :]:
            send_rows(to_layer)

    second_in[layer] = second_out[layer]
    second_got[layer] = second_stat[0]
    wait_all(second_out, second_in, LAYERS - 1, second_send, second_recv)
    wait_all(second_got, second_got, LAYERS - 1, second_stat_send, second_stat_recv)
    factors, _, total = join([second_got[i] for i in range(LAYERS)])
    hot = iota((8, HD), 1) == layer * 8 + iota((8, HD), 0)
    acc = None
    for i in range(LAYERS):
        term = second_in[i] * as_column(factors[i : i + 1], hot)
        acc = term if acc is None else acc + term
    normed = acc / as_column(total, hot)
    high = normed.astype(BF16)
    remain = normed - high.astype(F32)
    middle = remain.astype(BF16)
    low = (remain - middle.astype(F32)).astype(BF16)
    turned = (dot(low, signs) + dot(middle, signs) + dot(high, signs)) * root
    att_ref[0] = turned[0:STEPS].astype(BF16)
    att_ref[1] = turned[STEPS : 2 * STEPS].astype(BF16)

    far_copy.wait_send()
    keep.wait()
    wait_all(send, land_hbm, SEQ - 1, a2a_send, a2a_recv)


def finish_kernel(land_hbm, got_hbm, att_hbm, app_hbm, land, app, in_sems, out_sems, att_sem):
    att_copy = pltpu.make_async_copy(got_hbm, att_hbm, att_sem)
    att_copy.start()
    chunks = SEQ // 8
    for c in range(chunks):
        pltpu.make_async_copy(
            land_hbm.at[pl.ds(c * 8, 8)], land.at[pl.ds(c * 8, 8)], in_sems.at[c]
        ).start()
    to = iota((128, 128), 0)
    request, quarter = to // 64, lax.rem(to // 16, 4)
    source, rank = lax.rem(to // 2, 8), lax.rem(to, 2)
    wanted = source * 16 + request * 8 + quarter * 2 + rank
    move = jnp.where(iota((128, 128), 1) == wanted, 1.0, 0.0).astype(BF16)

    def out_copy(c):
        rows = pl.ds(c * 16, 16)
        return pltpu.make_async_copy(app.at[:, rows, :], app_hbm.at[:, rows, :], out_sems.at[c])

    for c in range(chunks):
        pltpu.make_async_copy(
            land_hbm.at[pl.ds(c * 8, 8)], land.at[pl.ds(c * 8, 8)], in_sems.at[c]
        ).wait()
        block = land[c * 8 : (c + 1) * 8].reshape(128, PIECE)
        moved = dot(move, block).astype(BF16)
        for r in range(REQ):
            for q in range(4):
                start = r * 64 + q * 16
                app[r, c * 16 : (c + 1) * 16, q * PIECE : (q + 1) * PIECE] = moved[start : start + 16]
        out_copy(c).start()
    for c in range(chunks):
        out_copy(c).wait()
    att_copy.wait()


def local(queries, cache_levels, scale_ids, scale_table, ctx_len, span_rows, span_len, owners):
    vmem, smem = pl.BlockSpec(memory_space=pltpu.VMEM), pl.BlockSpec(memory_space=pltpu.SMEM)
    anywhere = pl.BlockSpec(memory_space=pl.ANY)
    dma = pltpu.SemaphoreType.DMA
    turn = lambda x: jnp.swapaxes(x, -1, -2)
    landed, attended = pl.pallas_call(
        exchange_kernel,
        out_shape=(
            jax.ShapeDtypeStruct((SEQ, 16, PIECE), BF16),
            jax.ShapeDtypeStruct((REQ, STEPS, HD), BF16),
        ),
        in_specs=[anywhere, anywhere, smem, anywhere, smem, anywhere, smem, vmem],
        out_specs=(anywhere, vmem),
        scratch_shapes=[
            pltpu.VMEM((REQ, STEPS, HQ * HD), BF16),
            pltpu.VMEM((REQ, SLOT, WIDTH), BF16),
            pltpu.VMEM((REQ, SPAN, WIDTH), BF16),
            pltpu.VMEM((SEQ, 16, PIECE), BF16),
            pltpu.VMEM((2, BATCH_Y, NSCALE, 256), F32),
            pltpu.VMEM((2, BATCH_Y, REQ * (SLOT // GROUP), 256), F32),
            pltpu.VMEM((HQ * 8, HD), BF16),
            pltpu.VMEM((64, REQ * (SLOT + SPAN)), F32),
            pltpu.VMEM((PLANE, 64, HD), F32),
            pltpu.VMEM((PLANE, 64, HD), F32),
            pltpu.VMEM((PLANE, 2, HD), F32),
            pltpu.VMEM((PLANE, 2, HD), F32),
            pltpu.VMEM((LAYERS, 8, HD), F32),
            pltpu.VMEM((LAYERS, 8, HD), F32),
            pltpu.VMEM((1, 2, HD), F32),
            pltpu.VMEM((LAYERS, 2, HD), F32),
        ]
        + [dma] * 21
        + [pltpu.SemaphoreType.REGULAR((LAYERS,))],
        compiler_params=pltpu.CompilerParams(
            collective_id=0, has_side_effects=True, vmem_limit_bytes=VMEM
        ),
        cost_estimate=pl.CostEstimate(
            flops=2 * 10**9, bytes_accessed=5 * 2**20, transcendentals=400000
        ),
        name="exchange",
    )(
        queries, cache_levels, scale_ids, scale_table,
        turn(ctx_len), span_rows, turn(span_len), turn(owners),
    )
    return pl.pallas_call(
        finish_kernel,
        out_shape=(
            jax.ShapeDtypeStruct((REQ, STEPS, HD), BF16),
            jax.ShapeDtypeStruct((REQ, SEQ * CAP, WIDTH), BF16),
        ),
        in_specs=[anywhere, anywhere],
        out_specs=(anywhere, anywhere),
        scratch_shapes=[
            pltpu.VMEM((SEQ, 16, PIECE), BF16),
            pltpu.VMEM((REQ, SEQ * CAP, WIDTH), BF16),
            dma((8,)),
            dma((8,)),
            dma,
        ],
        compiler_params=pltpu.CompilerParams(vmem_limit_bytes=VMEM),
        name="finish",
    )(landed, attended)


def solution(mesh):
    return jax.shard_map(
        local,
        mesh=mesh,
        in_specs=(
            P("batch", None, None),
            P("batch", "seq", None),
            P("batch", "seq"),
            P(None, "batch"),
            P("batch", "seq"),
            P("batch", "seq", None),
            P("batch", "seq"),
            P("batch", "seq", None),
        ),
        out_specs=(P("batch", None, "seq"), P("batch", "seq", None)),
        check_vma=False,
    )
```

time: 80.8 us -> 70 us (0.87)
  the two profiles are of different devices: /device:TPU:1 before, /device:TPU:65 now
where the time goes in v2:
time: 70 us; the launch traced here: 69.8 us
  Pallas kernels  69.1 us (99%)
    pallas_call x1, Pallas kernels, local(): pl.pallas_call(exchange_kernel, out_shape=(jax.ShapeDtypeStruct((SEQ, 16,...  66 us
    pallas_call x1, Pallas kernels, local(): pl.pallas_call(finish_kernel, out_shape=(jax.ShapeDtypeStruct((REQ, STEPS...  3.11 us

profile of v2, /device:TPU:65, one launch (start us, length us, event | category | flops | bytes accessed | tf_op | source)
XLA Modules:
  0.0 69.8 jit_solution(11593468061568447888)
XLA Ops:
  0.6 66.0 %exchange.1 = (bf16[64,16,512]{2,1,0:T(8,128)(2,1)}, bf16[2,4,128]{2,1,0:T(4,128)(2,1)}) custom-call(bf16[2,4,8192]{2,1,0:T(4,128)(2,1)} %q_hbm.1, bf16[2,256,2048]{2,1,0:T(8,128)(2,1)} %lev_hbm.1, s32[2,8]{1,0:T(2,128)} %ids_ref.1, f32[16,256]{1,0:T(8,128)} %tab_hbm.1, s32[1,2]{1,0:T(1,128)} %bitcast.6, bf16[2,64,2048]{2,1,0:T(8,128)(2,1)} %span_hbm.1, ...), custom_call_target="tpu_custom_call" | custom-call | flops 2000000000 | bytes 5242880 | tf_op jit(solution)/shard_map/exchange/pallas_call | solution.py:421
  66.7 3.1 %finish.1 = (bf16[2,4,128]{2,1,0:T(4,128)(2,1)}, bf16[2,128,2048]{2,1,0:T(8,128)(2,1)}) custom-call(bf16[64,16,512]{2,1,0:T(8,128)(2,1)} %get-tuple-element.4.land_hbm, bf16[2,4,128]{2,1,0:T(4,128)(2,1)} %get-tuple-element.5.got_hbm), custom_call_target="tpu_custom_call" | custom-call | tf_op jit(solution)/shard_map/finish/pallas_call | solution.py:460

commit v3 on v2

--- a/solution.py
+++ b/solution.py
@@ -59,15 +59,16 @@
 
 
 def exchange_kernel(
-    q_hbm, lev_hbm, ids_ref, tab_hbm, ctx_ref, span_hbm, slen_ref, own_ref,
-    land_hbm, att_ref,
+    q_hbm, lev_hbm, ids_hbm, tab_hbm, ctx_hbm, span_hbm, slen_hbm, own_hbm,
+    land_hbm, att_hbm,
+    ids_ref, ctx_ref, slen_ref, own_ref, att_ref,
     q_ref, lev, span, send, tbl, scales, qrot, mask,
     first_out, first_in, first_stat, first_got, second_out, second_in, second_stat, second_got,
-    q_sem, tab_sem, lev_sem, span_sem, own_sem,
+    small_sems, q_sem, tab_sem, lev_sem, span_sem, own_sem,
     a2a_send, a2a_recv, far_send, far_recv, near_send, near_recv, side_send, side_recv,
     first_send, first_recv, first_stat_send, first_stat_recv,
     second_send, second_recv, second_stat_send, second_stat_recv,
-    ready,
+    ready, joined,
 ):
     me = lax.axis_index("seq")
     layer, place = me // PLANE, lax.rem(me, PLANE)
@@ -92,9 +93,31 @@
     loop(1, PLANE, lambda i: greet({"seq": layer * PLANE + lax.rem(place + i, PLANE)}))
     for side in sides:
         greet({"batch": side})
-    pl.when(far == 0)(lambda: greet({"batch": partner}))
+
+    at_end = (layer == 0) | (layer == LAYERS - 1)
+    sender = {"seq": jnp.where(lower, LAYERS - 1, 0) * PLANE + place, "batch": partner}
+
+    def taker(i):
+        return {
+            "seq": (jnp.where(layer == 0, LAYERS // 2, 0) + i) * PLANE + place,
+            "batch": partner,
+        }
+
+    @pl.when(far == 0)
+    def _():
+        greet(sender)
+        pl.when(at_end)(lambda: loop(0, LAYERS // 2, lambda i: greet(taker(i))))
+
     loop((layer + 1) * PLANE, SEQ, lambda i: greet({"seq": i}))
 
+    small = [
+        pltpu.make_async_copy(here, there, small_sems.at[i])
+        for i, (here, there) in enumerate(
+            ((own_hbm, own_ref), (slen_hbm, slen_ref), (ctx_hbm, ctx_ref), (ids_hbm, ids_ref))
+        )
+    ]
+    for copy in small:
+        copy.start()
     span_copy = pltpu.make_async_copy(span_hbm, span, span_sem)
     span_copy.start()
     tab_copy = pltpu.make_async_copy(tab_hbm, tbl.at[far, row], tab_sem)
@@ -104,6 +127,8 @@
     lev_copy = pltpu.make_async_copy(lev_hbm, lev, lev_sem)
     lev_copy.start()
 
+    for copy in small:
+        copy.wait()
     owner_row = jnp.concatenate([own_ref[0], own_ref[1]], axis=1).astype(F32)
     above, along = iota((2 * SPAN, 2 * SPAN), 0), iota((2 * SPAN, 2 * SPAN), 1)
     owner_wide = jnp.broadcast_to(owner_row, (2 * SPAN, 2 * SPAN))
@@ -132,7 +157,8 @@
         block = dot(pick, stacked).astype(BF16)
         send[pl.ds(to_layer * PLANE, PLANE)] = block.reshape(PLANE, 16, PIECE)
 
-    pl.semaphore_wait(barrier, PLANE - 1 + BATCH_Y - 1 + far + layer * PLANE)
+    known = far * (1 + jnp.where(at_end, LAYERS // 2, 0))
+    pl.semaphore_wait(barrier, PLANE - 1 + BATCH_Y - 1 + layer * PLANE + known)
 
     loop(
         0,
@@ -143,11 +169,19 @@
     )
 
     tab_copy.wait()
-    far_copy = pltpu.make_async_remote_copy(
-        src_ref=tbl.at[far, row], dst_ref=tbl.at[far, row], send_sem=far_send, recv_sem=far_recv,
-        device_id={"batch": partner}, device_id_type=MESH,
-    )
-    pl.when(far == 1)(far_copy.start)
+    def to_other_half():
+        def one(i):
+            pltpu.make_async_remote_copy(
+                src_ref=tbl.at[far, row], dst_ref=tbl.at[far, row],
+                send_sem=far_send, recv_sem=far_recv, device_id=taker(i), device_id_type=MESH,
+            ).start()
+
+        loop(0, LAYERS // 2, one)
+
+    @pl.when(far == 1)
+    def _():
+        pl.when(at_end)(to_other_half)
+        pl.semaphore_signal(joined, inc=1, device_id=sender, device_id_type=MESH)
 
     def to_sides(half, send_sem, recv_sem):
         for side in sides:
@@ -186,21 +220,36 @@
         send_rows(to_layer)
 
     half = LAYERS // 2
-    base = layer // half * half
-    across = [jnp.where(lower, half + i, half - 1 - i) for i in (0, 3, 1, 2)]
-    beside = [base + lax.rem(layer + i, half) for i in range(1, half)]
-
-    rest = [across[2], beside[0], beside[1], across[3], beside[2]]
-    post(across[0])
-    post(across[1])
+    own = jnp.where(lower, layer, LAYERS - 1 - layer)
+
+    def counted(number):
+        return jnp.where(lower, number, LAYERS - 1 - number)
+
+    across = [counted(half + i) for i in (0, 3, 1, 2)]
+
+    def post_inner():
+        for number in range(half - 1, 0, -1):
+            pl.when(number > own)(functools.partial(post, counted(number)))
+
+    def post_outer():
+        for number in range(half - 2, -1, -1):
+            pl.when(number < own)(functools.partial(post, counted(number)))
+
+    def post_some(layers):
+        for to_layer in layers:
+            post(to_layer)
+
+    post_inner()
+    post_some(across)
     send_rows(layer, 1)
+    post_outer()
     keep = pltpu.make_async_copy(send.at[me], land_hbm.at[me], own_sem)
     keep.start()
 
-    @pl.when(far == 1)
+    @pl.when((far == 0) & at_end)
     def _():
-        for to_layer in rest[: 5]:
-            post(to_layer)
+        pl.semaphore_wait(joined, LAYERS // 2)
+        to_other_half()
 
     signs = hadamard_signs()
     root = jnp.float32(1.0) / jnp.sqrt(jnp.float32(HD))
@@ -233,14 +282,10 @@
             group = jnp.where(here, ids_ref[r, b], group)
     chosen = jnp.where(lax.rem(iota((blocks, 3 * NSCALE), 1), NSCALE) == group, 1.0, 0.0).astype(BF16)
 
-    far_copy.wait_recv()
-
-    @pl.when(far == 0)
-    def _():
-        far_copy.start()
-        for to_layer in rest[: 3]:
-            post(to_layer)
-
+    pltpu.make_async_remote_copy(
+        src_ref=tbl.at[0, 0], dst_ref=tbl.at[0, 0], send_sem=far_send, recv_sem=far_recv,
+        device_id={"batch": partner}, device_id_type=MESH,
+    ).wait_recv()
     to_sides(1 - far, side_send, side_recv)
     from_sides(near_send, near_recv)
     from_sides(side_send, side_recv)
@@ -343,18 +388,7 @@
                 device_id={"seq": to * PLANE + place}, device_id_type=MESH,
             ).start()
 
-    @pl.when(far == 0)
-    def _():
-        for to_layer in rest[3 :]:
-            await_layer(to_layer)
-
     loop(1, LAYERS, second_post)
-
-    @pl.when(far == 0)
-    def _():
-        for to_layer in rest[3 :]:
-            send_rows(to_layer)
-
     second_in[layer] = second_out[layer]
     second_got[layer] = second_stat[0]
     wait_all(second_out, second_in, LAYERS - 1, second_send, second_recv)
@@ -373,8 +407,15 @@
     turned = (dot(low, signs) + dot(middle, signs) + dot(high, signs)) * root
     att_ref[0] = turned[0:STEPS].astype(BF16)
     att_ref[1] = turned[STEPS : 2 * STEPS].astype(BF16)
-
-    far_copy.wait_send()
+    att_copy = pltpu.make_async_copy(att_ref, att_hbm, small_sems.at[0])
+    att_copy.start()
+
+    sent = pltpu.make_async_remote_copy(
+        src_ref=tbl.at[0], dst_ref=tbl.at[0], send_sem=far_send, recv_sem=far_recv,
+        device_id={"batch": partner}, device_id_type=MESH,
+    )
+    pl.when(at_end)(sent.wait_send)
+    att_copy.wait()
     keep.wait()
     wait_all(send, land_hbm, SEQ - 1, a2a_send, a2a_recv)
 
@@ -414,7 +455,6 @@
 
 
 def local(queries, cache_levels, scale_ids, scale_table, ctx_len, span_rows, span_len, owners):
-    vmem, smem = pl.BlockSpec(memory_space=pltpu.VMEM), pl.BlockSpec(memory_space=pltpu.SMEM)
     anywhere = pl.BlockSpec(memory_space=pl.ANY)
     dma = pltpu.SemaphoreType.DMA
     turn = lambda x: jnp.swapaxes(x, -1, -2)
@@ -424,9 +464,14 @@
             jax.ShapeDtypeStruct((SEQ, 16, PIECE), BF16),
             jax.ShapeDtypeStruct((REQ, STEPS, HD), BF16),
         ),
-        in_specs=[anywhere, anywhere, smem, anywhere, smem, anywhere, smem, vmem],
-        out_specs=(anywhere, vmem),
+        in_specs=[anywhere] * 8,
+        out_specs=(anywhere, anywhere),
         scratch_shapes=[
+            pltpu.SMEM((REQ, SLOT // GROUP), jnp.int32),
+            pltpu.SMEM((1, REQ), jnp.int32),
+            pltpu.SMEM((1, REQ), jnp.int32),
+            pltpu.VMEM((REQ, 1, SPAN), jnp.int32),
+            pltpu.VMEM((REQ, STEPS, HD), BF16),
             pltpu.VMEM((REQ, STEPS, HQ * HD), BF16),
             pltpu.VMEM((REQ, SLOT, WIDTH), BF16),
             pltpu.VMEM((REQ, SPAN, WIDTH), BF16),
@@ -444,8 +489,9 @@
             pltpu.VMEM((1, 2, HD), F32),
             pltpu.VMEM((LAYERS, 2, HD), F32),
         ]
+        + [dma((4,))]
         + [dma] * 21
-        + [pltpu.SemaphoreType.REGULAR((LAYERS,))],
+        + [pltpu.SemaphoreType.REGULAR((LAYERS,)), pltpu.SemaphoreType.REGULAR],
         compiler_params=pltpu.CompilerParams(
             collective_id=0, has_side_effects=True, vmem_limit_bytes=VMEM
         ),

time: 70 us -> 65.5 us (0.936)
  the two profiles are of different devices: /device:TPU:65 before, /device:TPU:1 now
where the time goes in v3:
time: 65.5 us; the launch traced here: 65.3 us
  Pallas kernels  64.7 us (99%)
    pallas_call x1, Pallas kernels, local(): pl.pallas_call(exchange_kernel, out_shape=(jax.ShapeDtypeStruct((SEQ, 16,...  61.6 us
    pallas_call x1, Pallas kernels, local(): pl.pallas_call(finish_kernel, out_shape=(jax.ShapeDtypeStruct((REQ, STEPS...  3.11 us

profile of v3, /device:TPU:1, one launch (start us, length us, event | category | flops | bytes accessed | tf_op | source)
XLA Modules:
  0.0 65.3 jit_solution(2581638416680443682)
XLA Ops:
  0.6 61.6 %exchange.1 = (bf16[64,16,512]{2,1,0:T(8,128)(2,1)}, bf16[2,4,128]{2,1,0:T(4,128)(2,1)}) custom-call(bf16[2,4,8192]{2,1,0:T(4,128)(2,1)} %q_hbm.1, bf16[2,256,2048]{2,1,0:T(8,128)(2,1)} %lev_hbm.1, s32[2,8]{1,0:T(2,128)} %ids_hbm.1, f32[16,256]{1,0:T(8,128)} %tab_hbm.1, s32[1,2]{1,0:T(1,128)} %bitcast.6, bf16[2,64,2048]{2,1,0:T(8,128)(2,1)} %span_hbm.1, ...), custom_call_target="tpu_custom_call" | custom-call | flops 2000000000 | bytes 5242880 | tf_op jit(solution)/shard_map/exchange/pallas_call | solution.py:461
  62.2 3.1 %finish.1 = (bf16[2,4,128]{2,1,0:T(4,128)(2,1)}, bf16[2,128,2048]{2,1,0:T(8,128)(2,1)}) custom-call(bf16[64,16,512]{2,1,0:T(8,128)(2,1)} %get-tuple-element.4.land_hbm, bf16[2,4,128]{2,1,0:T(4,128)(2,1)} %get-tuple-element.5.got_hbm), custom_call_target="tpu_custom_call" | custom-call | tf_op jit(solution)/shard_map/finish/pallas_call | solution.py:506

commit v4 on v3

--- a/solution.py
+++ b/solution.py
@@ -60,11 +60,11 @@
 
 def exchange_kernel(
     q_hbm, lev_hbm, ids_hbm, tab_hbm, ctx_hbm, span_hbm, slen_hbm, own_hbm,
-    land_hbm, att_hbm,
-    ids_ref, ctx_ref, slen_ref, own_ref, att_ref,
+    app_hbm, att_hbm,
+    land, app, ids_ref, ctx_ref, slen_ref, own_ref, att_ref,
     q_ref, lev, span, send, tbl, scales, qrot, mask,
     first_out, first_in, first_stat, first_got, second_out, second_in, second_stat, second_got,
-    small_sems, q_sem, tab_sem, lev_sem, span_sem, own_sem,
+    small_sems, q_sem, tab_sem, lev_sem, span_sem, app_sems,
     a2a_send, a2a_recv, far_send, far_recv, near_send, near_recv, side_send, side_recv,
     first_send, first_recv, first_stat_send, first_stat_recv,
     second_send, second_recv, second_stat_send, second_stat_recv,
@@ -109,6 +109,7 @@
         pl.when(at_end)(lambda: loop(0, LAYERS // 2, lambda i: greet(taker(i))))
 
     loop((layer + 1) * PLANE, SEQ, lambda i: greet({"seq": i}))
+    pl.when(far == 1)(lambda: loop(0, layer * PLANE, lambda i: greet({"seq": i})))
 
     small = [
         pltpu.make_async_copy(here, there, small_sems.at[i])
@@ -158,11 +159,12 @@
         send[pl.ds(to_layer * PLANE, PLANE)] = block.reshape(PLANE, 16, PIECE)
 
     known = far * (1 + jnp.where(at_end, LAYERS // 2, 0))
-    pl.semaphore_wait(barrier, PLANE - 1 + BATCH_Y - 1 + layer * PLANE + known)
+    layers_known = jnp.where(far == 0, layer, LAYERS - 1)
+    pl.semaphore_wait(barrier, PLANE - 1 + BATCH_Y - 1 + layers_known * PLANE + known)
 
     loop(
         0,
-        layer,
+        jnp.where(far == 0, layer, 0),
         lambda i: pl.semaphore_signal(
             ready.at[layer], inc=1, device_id={"seq": i * PLANE + place}, device_id_type=MESH
         ),
@@ -203,13 +205,13 @@
     to_sides(far, near_send, near_recv)
 
     def await_layer(to_layer):
-        pl.when(to_layer > layer)(lambda: pl.semaphore_wait(ready.at[to_layer], 1))
+        pl.when((to_layer > layer) & (far == 0))(lambda: pl.semaphore_wait(ready.at[to_layer], 1))
 
     def send_rows(to_layer, start=0):
         def one(i):
             to = to_layer * PLANE + lax.rem(place + i, PLANE)
             pltpu.make_async_remote_copy(
-                src_ref=send.at[to], dst_ref=land_hbm.at[me], send_sem=a2a_send, recv_sem=a2a_recv,
+                src_ref=send.at[to], dst_ref=land.at[me], send_sem=a2a_send, recv_sem=a2a_recv.at[layer],
                 device_id={"seq": to}, device_id_type=MESH,
             ).start()
 
@@ -225,26 +227,28 @@
     def counted(number):
         return jnp.where(lower, number, LAYERS - 1 - number)
 
-    across = [counted(half + i) for i in (0, 3, 1, 2)]
+    across = [
+        jnp.where(lower, half + up, half - 1 - jnp.where(far == 0, down, other))
+        for up, down, other in zip((0, 3, 2, 1), (3, 2, 1, 0), (0, 3, 2, 1))
+    ]
 
     def post_inner():
         for number in range(half - 1, 0, -1):
             pl.when(number > own)(functools.partial(post, counted(number)))
 
-    def post_outer():
+    def each_outer(act):
         for number in range(half - 2, -1, -1):
-            pl.when(number < own)(functools.partial(post, counted(number)))
+            pl.when(number < own)(functools.partial(act, counted(number)))
 
     def post_some(layers):
         for to_layer in layers:
             post(to_layer)
 
     post_inner()
-    post_some(across)
+    post_some(across[: 3])
     send_rows(layer, 1)
-    post_outer()
-    keep = pltpu.make_async_copy(send.at[me], land_hbm.at[me], own_sem)
-    keep.start()
+    each_outer(post)
+    land[me] = send[me]
 
     @pl.when((far == 0) & at_end)
     def _():
@@ -388,9 +392,43 @@
                 device_id={"seq": to * PLANE + place}, device_id_type=MESH,
             ).start()
 
+    for to_layer in across[3 :]:
+        await_layer(to_layer)
     loop(1, LAYERS, second_post)
+    for to_layer in across[3 :]:
+        send_rows(to_layer)
     second_in[layer] = second_out[layer]
     second_got[layer] = second_stat[0]
+    to = iota((128, 128), 0)
+    request, quarter = to // 64, lax.rem(to // 16, 4)
+    source, rank = lax.rem(to // 2, 8), lax.rem(to, 2)
+    wanted = source * 16 + request * 8 + quarter * 2 + rank
+    move = jnp.where(iota((128, 128), 1) == wanted, 1.0, 0.0).astype(BF16)
+
+    def out_copy(at):
+        rows = pl.ds(pl.multiple_of(at * 16, 16), 16)
+        return pltpu.make_async_copy(app.at[:, rows, :], app_hbm.at[:, rows, :], app_sems.at[at])
+
+    def place_layer(at, count):
+        some = land.at[pl.ds(0, count)]
+        pltpu.make_async_remote_copy(
+            src_ref=some, dst_ref=some, send_sem=a2a_send, recv_sem=a2a_recv.at[at],
+            device_id={"seq": me}, device_id_type=MESH,
+        ).wait_recv()
+        block = land[pl.ds(at * PLANE, PLANE)].reshape(128, PIECE)
+        moved = dot(move, block).astype(BF16)
+        rows = pl.ds(pl.multiple_of(at * 16, 16), 16)
+        for r in range(REQ):
+            for q in range(4):
+                start = r * 64 + q * 16
+                app[r, rows, q * PIECE : (q + 1) * PIECE] = moved[start : start + 16]
+        out_copy(at).start()
+
+    place_layer(layer, PLANE - 1)
+    for i in range(1, half):
+        place_layer(layer // half * half + lax.rem(layer + i, half), PLANE)
+    for i in range(half):
+        place_layer(counted(LAYERS - 1 - i), PLANE)
     wait_all(second_out, second_in, LAYERS - 1, second_send, second_recv)
     wait_all(second_got, second_got, LAYERS - 1, second_stat_send, second_stat_recv)
     factors, _, total = join([second_got[i] for i in range(LAYERS)])
@@ -416,41 +454,31 @@
     )
     pl.when(at_end)(sent.wait_send)
     att_copy.wait()
-    keep.wait()
-    wait_all(send, land_hbm, SEQ - 1, a2a_send, a2a_recv)
-
-
-def finish_kernel(land_hbm, got_hbm, att_hbm, app_hbm, land, app, in_sems, out_sems, att_sem):
+
+    loop(0, LAYERS, lambda at: out_copy(at).wait())
+    rows_sent = send.at[pl.ds(0, SEQ - 1)]
+    pltpu.make_async_remote_copy(
+        src_ref=rows_sent, dst_ref=rows_sent, send_sem=a2a_send, recv_sem=far_recv,
+        device_id={"seq": me}, device_id_type=MESH,
+    ).wait_send()
+
+
+def finish_kernel(app_hbm, got_hbm, att_hbm, out_hbm, app, in_sems, out_sems, att_sem):
     att_copy = pltpu.make_async_copy(got_hbm, att_hbm, att_sem)
     att_copy.start()
-    chunks = SEQ // 8
+    chunks, rows = 4, SEQ * CAP // 4
+    ins, outs = [], []
     for c in range(chunks):
-        pltpu.make_async_copy(
-            land_hbm.at[pl.ds(c * 8, 8)], land.at[pl.ds(c * 8, 8)], in_sems.at[c]
-        ).start()
-    to = iota((128, 128), 0)
-    request, quarter = to // 64, lax.rem(to // 16, 4)
-    source, rank = lax.rem(to // 2, 8), lax.rem(to, 2)
-    wanted = source * 16 + request * 8 + quarter * 2 + rank
-    move = jnp.where(iota((128, 128), 1) == wanted, 1.0, 0.0).astype(BF16)
-
-    def out_copy(c):
-        rows = pl.ds(c * 16, 16)
-        return pltpu.make_async_copy(app.at[:, rows, :], app_hbm.at[:, rows, :], out_sems.at[c])
-
-    for c in range(chunks):
-        pltpu.make_async_copy(
-            land_hbm.at[pl.ds(c * 8, 8)], land.at[pl.ds(c * 8, 8)], in_sems.at[c]
-        ).wait()
-        block = land[c * 8 : (c + 1) * 8].reshape(128, PIECE)
-        moved = dot(move, block).astype(BF16)
-        for r in range(REQ):
-            for q in range(4):
-                start = r * 64 + q * 16
-                app[r, c * 16 : (c + 1) * 16, q * PIECE : (q + 1) * PIECE] = moved[start : start + 16]
-        out_copy(c).start()
-    for c in range(chunks):
-        out_copy(c).wait()
+        part = (slice(None), pl.ds(c * rows, rows))
+        ins.append(pltpu.make_async_copy(app_hbm.at[part], app.at[part], in_sems.at[c]))
+        outs.append(pltpu.make_async_copy(app.at[part], out_hbm.at[part], out_sems.at[c]))
+    for copy in ins:
+        copy.start()
+    for into, out in zip(ins, outs):
+        into.wait()
+        out.start()
+    for copy in outs:
+        copy.wait()
     att_copy.wait()
 
 
@@ -458,15 +486,17 @@
     anywhere = pl.BlockSpec(memory_space=pl.ANY)
     dma = pltpu.SemaphoreType.DMA
     turn = lambda x: jnp.swapaxes(x, -1, -2)
-    landed, attended = pl.pallas_call(
+    appended, attended = pl.pallas_call(
         exchange_kernel,
         out_shape=(
-            jax.ShapeDtypeStruct((SEQ, 16, PIECE), BF16),
+            jax.ShapeDtypeStruct((REQ, SEQ * CAP, WIDTH), BF16),
             jax.ShapeDtypeStruct((REQ, STEPS, HD), BF16),
         ),
         in_specs=[anywhere] * 8,
         out_specs=(anywhere, anywhere),
         scratch_shapes=[
+            pltpu.VMEM((SEQ, 16, PIECE), BF16),
+            pltpu.VMEM((REQ, SEQ * CAP, WIDTH), BF16),
             pltpu.SMEM((REQ, SLOT // GROUP), jnp.int32),
             pltpu.SMEM((1, REQ), jnp.int32),
             pltpu.SMEM((1, REQ), jnp.int32),
@@ -490,7 +520,9 @@
             pltpu.VMEM((LAYERS, 2, HD), F32),
         ]
         + [dma((4,))]
-        + [dma] * 21
+        + [dma] * 4
+        + [dma((LAYERS,)), dma, dma((LAYERS,))]
+        + [dma] * 14
         + [pltpu.SemaphoreType.REGULAR((LAYERS,)), pltpu.SemaphoreType.REGULAR],
         compiler_params=pltpu.CompilerParams(
             collective_id=0, has_side_effects=True, vmem_limit_bytes=VMEM
@@ -512,15 +544,14 @@
         in_specs=[anywhere, anywhere],
         out_specs=(anywhere, anywhere),
         scratch_shapes=[
-            pltpu.VMEM((SEQ, 16, PIECE), BF16),
             pltpu.VMEM((REQ, SEQ * CAP, WIDTH), BF16),
-            dma((8,)),
-            dma((8,)),
+            dma((4,)),
+            dma((4,)),
             dma,
         ],
         compiler_params=pltpu.CompilerParams(vmem_limit_bytes=VMEM),
         name="finish",
-    )(landed, attended)
+    )(appended, attended)
 
 
 def solution(mesh):

time: 65.5 us -> 64.4 us (0.983)
  Pallas kernels: 64.7 us -> 63.6 us
    pallas_call x1, Pallas kernels: 3.11 us -> 1.99 us  [local(): pl.pallas_call(finish_kernel, out_shape=(jax.ShapeDtypeStruct((REQ, STEPS...]
where the time goes in v4:
time: 64.4 us; the launch traced here: 64.3 us
  Pallas kernels  63.6 us (99%)
    pallas_call x1, Pallas kernels, local(): pl.pallas_call(exchange_kernel, out_shape=(jax.ShapeDtypeStruct((REQ, SEQ...  61.6 us
    pallas_call x1, Pallas kernels, local(): pl.pallas_call(finish_kernel, out_shape=(jax.ShapeDtypeStruct((REQ, STEPS...  1.99 us

profile of v4, /device:TPU:1, one launch (start us, length us, event | category | flops | bytes accessed | tf_op | source)
XLA Modules:
  0.0 64.3 jit_solution(11188397902076849506)
XLA Ops:
  0.6 61.6 %exchange.1 = (bf16[2,128,2048]{2,1,0:T(8,128)(2,1)}, bf16[2,4,128]{2,1,0:T(4,128)(2,1)}) custom-call(bf16[2,4,8192]{2,1,0:T(4,128)(2,1)} %q_hbm.1, bf16[2,256,2048]{2,1,0:T(8,128)(2,1)} %lev_hbm.1, s32[2,8]{1,0:T(2,128)} %ids_hbm.1, f32[16,256]{1,0:T(8,128)} %tab_hbm.1, s32[1,2]{1,0:T(1,128)} %bitcast.6, bf16[2,64,2048]{2,1,0:T(8,128)(2,1)} %span_hbm.1, ...), custom_call_target="tpu_custom_call" | custom-call | flops 2000000000 | bytes 5242880 | tf_op jit(solution)/shard_map/exchange/pallas_call | solution.py:489
  62.3 2.0 %finish.1 = (bf16[2,4,128]{2,1,0:T(4,128)(2,1)}, bf16[2,128,2048]{2,1,0:T(8,128)(2,1)}) custom-call(bf16[2,128,2048]{2,1,0:T(8,128)(2,1)} %get-tuple-element.4.app_hbm, bf16[2,4,128]{2,1,0:T(4,128)(2,1)} %get-tuple-element.5.got_hbm), custom_call_target="tpu_custom_call" | custom-call | tf_op jit(solution)/shard_map/finish/pallas_call | solution.py:538

commit v5 on v4

--- a/solution.py
+++ b/solution.py
@@ -245,7 +245,9 @@
             post(to_layer)
 
     post_inner()
-    post_some(across[: 3])
+    hold = (own < 2) & (far == 0)
+    post_some(across[:2])
+    pl.when(jnp.logical_not(hold))(lambda: post(across[2]))
     send_rows(layer, 1)
     each_outer(post)
     land[me] = send[me]
@@ -392,9 +394,11 @@
                 device_id={"seq": to * PLANE + place}, device_id_type=MESH,
             ).start()
 
+    pl.when(hold)(lambda: await_layer(across[2]))
     for to_layer in across[3 :]:
         await_layer(to_layer)
     loop(1, LAYERS, second_post)
+    pl.when(hold)(lambda: send_rows(across[2]))
     for to_layer in across[3 :]:
         send_rows(to_layer)
     second_in[layer] = second_out[layer]

time: 64.4 us -> 64.5 us (level)
  no operation moved by 1% of the time
where the time goes in v5:
time: 64.5 us; the launch traced here: 64.3 us
  Pallas kernels  63.7 us (99%)
    pallas_call x1, Pallas kernels, local(): pl.pallas_call(exchange_kernel, out_shape=(jax.ShapeDtypeStruct((REQ, SEQ...  61.7 us
    pallas_call x1, Pallas kernels, local(): pl.pallas_call(finish_kernel, out_shape=(jax.ShapeDtypeStruct((REQ, STEPS...  1.99 us

profile of v5, /device:TPU:1, one launch (start us, length us, event | category | flops | bytes accessed | tf_op | source)
XLA Modules:
  0.0 64.3 jit_solution(15910228475228840632)
XLA Ops:
  0.6 61.7 %exchange.1 = (bf16[2,128,2048]{2,1,0:T(8,128)(2,1)}, bf16[2,4,128]{2,1,0:T(4,128)(2,1)}) custom-call(bf16[2,4,8192]{2,1,0:T(4,128)(2,1)} %q_hbm.1, bf16[2,256,2048]{2,1,0:T(8,128)(2,1)} %lev_hbm.1, s32[2,8]{1,0:T(2,128)} %ids_hbm.1, f32[16,256]{1,0:T(8,128)} %tab_hbm.1, s32[1,2]{1,0:T(1,128)} %bitcast.6, bf16[2,64,2048]{2,1,0:T(8,128)(2,1)} %span_hbm.1, ...), custom_call_target="tpu_custom_call" | custom-call | flops 2000000000 | bytes 5242880 | tf_op jit(solution)/shard_map/exchange/pallas_call | solution.py:493
  62.3 2.0 %finish.1 = (bf16[2,4,128]{2,1,0:T(4,128)(2,1)}, bf16[2,128,2048]{2,1,0:T(8,128)(2,1)}) custom-call(bf16[2,128,2048]{2,1,0:T(8,128)(2,1)} %get-tuple-element.4.app_hbm, bf16[2,4,128]{2,1,0:T(4,128)(2,1)} %get-tuple-element.5.got_hbm), custom_call_target="tpu_custom_call" | custom-call | tf_op jit(solution)/shard_map/finish/pallas_call | solution.py:542
